TPU v7x, 768 devices: a whole 4x8x12 slice. The times are simulated.
768 devices in a mesh: replica: 16 (over x_lo, y), expert: 48 (over x_hi, z, core).
Axes of the slice: x: 4 (x_hi: 2, x_lo: 2; x = x_hi * 2 + x_lo), y: 8, z: 12, core: 2. Of those that a mesh axis runs over, the one named last changes fastest.
Arguments:
- tokens: bfloat16 [16, 6144, 1024], P('replica', 'expert'), may hold values from -6 to 6
- expert_ids: int32 [16, 6144, 8], P('replica', 'expert'), may hold values from 0 to 95, all different within a row; in each aligned block of 64 rows (0 to 63, 64 to 127, ..., all dimensions but the last counted through in order) at most 7 rows name the same one
- hidden_grad: bfloat16 [16, 6144, 8, 384], P('replica', 'expert'), may hold values from -0.59765625 to 0.59765625
- gate_weight: bfloat16 [96, 1024, 384], P('expert'), may hold values from -0.1875 to 0.1875
- up_weight: bfloat16 [96, 1024, 384], P('expert'), may hold values from -0.1875 to 0.1875
- outer_params: float32 [384, 2048], P('expert'), may hold values from -6 to 6
- momentum: float32 [384, 2048], P('expert'), may hold values from -3 to 3
- inner_params: float32 [16, 384, 2048], P('replica', 'expert'), may hold values from -6 to 6
Outputs:
- gate_grad: bfloat16 [16, 96, 1024, 384], P('replica', 'expert')
- up_grad: bfloat16 [16, 96, 1024, 384], P('replica', 'expert')
- new_outer: float32 [384, 2048], P('expert')
- new_momentum: float32 [384, 2048], P('expert')
Inputs may be any that keep to these rules, and one draw needn't show every extreme that they name: `expert_ids`: each token names 8 different experts; among the 64 tokens of one block no expert is chosen more than 7 times, a bound that some block reaches.
All inputs are finite; a program needn't handle non-finite values.
Results may differ from a plain program's by a relative error of at most 0.012.
Values may be sent and summed in bfloat16 or wider, within the bound.
A program may use at most 64 MiB of HBM per device.

v0:
```python
import jax
import jax.numpy as jnp
from jax import lax
from jax.sharding import PartitionSpec as P

BLOCKS = 2


def slot_ranks(ids, count):
    hits = (ids[:, :, None] == jnp.arange(count, dtype=jnp.int32)[None, None, :]).astype(jnp.int32)
    chosen = jnp.sum(hits, axis=1)
    before = jnp.cumsum(chosen, axis=0) - chosen
    return jnp.sum(hits * before[:, None, :], axis=2)


def local(
    tokens, expert_ids, hidden_grad, gate_weight, up_weight, outer_params, momentum, inner_params
):
    groups = lax.axis_size("expert")
    local_count = gate_weight.shape[0]
    experts_all = local_count * groups
    width = tokens.shape[2]
    hidden = hidden_grad.shape[3]
    choose = expert_ids.shape[2]
    blk_rows = tokens.shape[1] // BLOCKS
    capacity = max(2, (5 * blk_rows * choose + 4 * experts_all - 1) // (4 * experts_all))
    parts_x = []
    parts_h = []
    for block in range(BLOCKS):
        begin = block * blk_rows
        block_ids = expert_ids[0, begin : begin + blk_rows]
        block_tok = tokens[0, begin : begin + blk_rows]
        block_grad = hidden_grad[0, begin : begin + blk_rows]
        slot = slot_ranks(block_ids, experts_all)
        flat = (block_ids * capacity + slot).reshape(-1)
        repeated = jnp.broadcast_to(block_tok[:, None, :], (blk_rows, choose, width)).reshape(
            -1, width
        )
        send_x = jnp.zeros((experts_all * capacity, width), jnp.bfloat16).at[flat].set(repeated)
        send_h = (
            jnp.zeros((experts_all * capacity, hidden), jnp.bfloat16)
            .at[flat]
            .set(block_grad.reshape(-1, hidden))
        )
        send_x = send_x.reshape(groups, local_count, capacity, width)
        send_h = send_h.reshape(groups, local_count, capacity, hidden)
        got_x, got_h = (
            lax.all_to_all(send_x, "expert", split_axis=0, concat_axis=2, tiled=True),
            lax.all_to_all(send_h, "expert", split_axis=0, concat_axis=2, tiled=True),
        )
        parts_x.append(got_x.reshape(local_count, groups * capacity, width))
        parts_h.append(got_h.reshape(local_count, groups * capacity, hidden))
    rows_x = jnp.concatenate(parts_x, axis=1)
    rows_h = jnp.concatenate(parts_h, axis=1)
    gate = jnp.einsum("erd,edf->erf", rows_x, gate_weight, preferred_element_type=jnp.float32)
    upval = jnp.einsum("erd,edf->erf", rows_x, up_weight, preferred_element_type=jnp.float32)
    sig = jax.nn.sigmoid(gate)
    cotangent = rows_h.astype(jnp.float32)
    gate_d = (cotangent * upval * sig * (1.0 + gate * (1.0 - sig))).astype(jnp.bfloat16)
    up_d = (cotangent * gate * sig).astype(jnp.bfloat16)
    gate_grad = jnp.einsum(
        "erd,erf->edf", rows_x, gate_d, preferred_element_type=jnp.float32
    ).astype(jnp.bfloat16)
    up_grad = jnp.einsum("erd,erf->edf", rows_x, up_d, preferred_element_type=jnp.float32).astype(
        jnp.bfloat16
    )
    replicas = lax.axis_size("replica")
    summed = lax.psum(inner_params[0].astype(jnp.bfloat16), "replica").astype(jnp.float32)
    delta = outer_params - summed / replicas
    new_momentum = 0.9 * momentum + delta
    new_outer = outer_params - 0.7 * (delta + 0.9 * new_momentum)
    return (gate_grad[None], up_grad[None], new_outer, new_momentum)


def solution(mesh):
    in_specs = (
        P("replica", "expert", None),
        P("replica", "expert", None),
        P("replica", "expert", None, None),
        P("expert", None, None),
        P("expert", None, None),
        P("expert", None),
        P("expert", None),
        P("replica", "expert", None),
    )
    out_specs = (
        P("replica", "expert", None, None),
        P("replica", "expert", None, None),
        P("expert", None),
        P("expert", None),
    )
    return jax.shard_map(local, mesh=mesh, in_specs=in_specs, out_specs=out_specs, check_vma=False)
```

profile of v0, /device:TPU:6, one launch (start us, length us, event | category | flops | bytes accessed | tf_op | source)
XLA Modules:
  0.0 234.0 jit_solution(2981352787399099997)
XLA Ops:
  0.6 0.0 copy-start
  0.6 0.9 slice_bitcast_fusion.2
  1.5 0.1 copy.42
  1.6 0.2 convert_reduce_fusion
  1.8 0.1 reduce_window_sum.18
  1.9 1.2 select_reduce_fusion
  3.1 0.1 reduce_sum.45
  3.2 0.1 copy.41
  3.3 0.1 mul.79
  3.4 2.9 %scatter_custom_fusion.3 = bf16[672,384]{1,0:T(8,128)(2,1)S(1)} fusion(s32[512]{0:T(512)S(1)} %bitcast.56, bf16[1,128,8,384]{3,2,1,0:T(8,128)(2,1)} %param.10, bf16[]{:T(256)} %constant.8.clone.1), kind=kCustom, calls=%fused_computation.29 | custom fusion | bytes 909824 | tf_op jit(solution)/shard_map/scatter | solution.py:43
  6.4 0.2 reshape.141
  6.5 1.2 copy.47
  7.7 18.5 %all-to-all-start.3 = ((bf16[48,2,7,384]{3,1,2,0:T(2,128)(2,1)}), bf16[48,2,7,384]{3,1,2,0:T(2,128)(2,1)S(1)}, u32[]{:S(2)}, u32[]{:S(2)}) async-start(bf16[48,2,7,384]{3,1,2,0:T(2,128)(2,1)} %copy.47), calls=%async_computation.3 | async-start | bytes 1032192 | tf_op jit(solution)/shard_map/all_to_all | solution.py:49
  26.2 0.1 copy.39
  26.3 0.2 convert_reduce_fusion.1
  26.5 0.1 reduce_window_sum.17
  26.6 1.2 select_reduce_fusion.1
  27.8 0.1 reduce_sum.42
  27.9 0.1 copy.38
  28.0 0.1 mul.75
  28.1 0.0 copy-start.5
  28.1 2.9 %scatter_custom_fusion.2 = bf16[672,384]{1,0:T(8,128)(2,1)S(1)} fusion(s32[512]{0:T(512)S(1)} %bitcast.58, bf16[1,128,8,384]{3,2,1,0:T(8,128)(2,1)} %param.10, bf16[]{:T(256)} %constant.8.clone.1), kind=kCustom, calls=%fused_computation.31 | custom fusion | bytes 909824 | tf_op jit(solution)/shard_map/scatter | solution.py:43
  31.1 0.2 reshape.139
  31.3 1.2 copy.46
  32.5 14.6 %all-to-all-done.3 = bf16[48,2,7,384]{3,1,2,0:T(2,128)(2,1)S(1)} async-done(((bf16[48,2,7,384]{3,1,2,0:T(2,128)(2,1)}), bf16[48,2,7,384]{3,1,2,0:T(2,128)(2,1)S(1)}, u32[]{:S(2)}, u32[]{:S(2)}) %all-to-all-start.3) | async-done | bytes 516128 | tf_op jit(solution)/shard_map/all_to_all | solution.py:49
  47.0 9.9 %all-to-all-start.2 = ((bf16[48,2,7,384]{3,1,2,0:T(2,128)(2,1)}), bf16[48,2,7,384]{3,1,2,0:T(2,128)(2,1)}, u32[]{:S(2)}, u32[]{:S(2)}) async-start(bf16[48,2,7,384]{3,1,2,0:T(2,128)(2,1)} %copy.46), calls=%async_computation.2 | async-start | bytes 1032192 | tf_op jit(solution)/shard_map/all_to_all | solution.py:49
  57.0 3.7 %scatter_custom_fusion = bf16[672,1024]{1,0:T(8,128)(2,1)} fusion(s32[512]{0:T(512)S(1)} %bitcast.59, bf16[]{:T(256)} %constant.8.clone.1, bf16[64,1024]{1,0:T(8,128)(2,1)S(1)} %get-tuple-element.7), kind=kCustom, calls=%fused_computation.20 | custom fusion | bytes 1507330 | tf_op jit(solution)/shard_map/scatter | solution.py:39
  60.7 2.3 reshape.134
  63.0 2.7 %copy.40 = bf16[48,2,7,1024]{3,1,2,0:T(2,128)(2,1)} copy(bf16[48,2,7,1024]{3,2,1,0:T(8,128)(2,1)S(1)} %reshape.134) | data formatting | bytes 2752512 | tf_op jit(solution)/shard_map/reshape | solution.py:45
  65.6 12.0 %all-to-all-done.2 = bf16[48,2,7,384]{3,1,2,0:T(2,128)(2,1)} async-done(((bf16[48,2,7,384]{3,1,2,0:T(2,128)(2,1)}), bf16[48,2,7,384]{3,1,2,0:T(2,128)(2,1)}, u32[]{:S(2)}, u32[]{:S(2)}) %all-to-all-start.2) | async-done | bytes 516128 | tf_op jit(solution)/shard_map/all_to_all | solution.py:49
  77.7 9.9 %all-to-all-start = ((bf16[48,2,7,1024]{3,1,2,0:T(2,128)(2,1)}), bf16[48,2,7,1024]{3,1,2,0:T(2,128)(2,1)}, u32[]{:S(2)}, u32[]{:S(2)}) async-start(bf16[48,2,7,1024]{3,1,2,0:T(2,128)(2,1)} %copy.40), calls=%async_computation | async-start | bytes 2752512 | tf_op jit(solution)/shard_map/all_to_all | solution.py:48
  87.6 3.7 %scatter_custom_fusion.1 = bf16[672,1024]{1,0:T(8,128)(2,1)} fusion(s32[512]{0:T(512)S(1)} %bitcast.57, bf16[]{:T(256)} %constant.8.clone.1, bf16[64,1024]{1,0:T(8,128)(2,1)S(1)} %get-tuple-element.6), kind=kCustom, calls=%fused_computation.18 | custom fusion | bytes 1507330 | tf_op jit(solution)/shard_map/scatter | solution.py:39
  91.3 2.3 reshape.137
  93.6 2.7 %copy.43 = bf16[48,2,7,1024]{3,1,2,0:T(2,128)(2,1)} copy(bf16[48,2,7,1024]{3,2,1,0:T(8,128)(2,1)S(1)} %reshape.137) | data formatting | bytes 2752512 | tf_op jit(solution)/shard_map/reshape | solution.py:45
  96.2 37.5 %all-to-all-done = bf16[48,2,7,1024]{3,1,2,0:T(2,128)(2,1)} async-done(((bf16[48,2,7,1024]{3,1,2,0:T(2,128)(2,1)}), bf16[48,2,7,1024]{3,1,2,0:T(2,128)(2,1)}, u32[]{:S(2)}, u32[]{:S(2)}) %all-to-all-start) | async-done | bytes 1376288 | tf_op jit(solution)/shard_map/all_to_all | solution.py:48
  133.8 12.0 %all-to-all-start.1 = ((bf16[48,2,7,1024]{3,1,2,0:T(2,128)(2,1)}), bf16[48,2,7,1024]{3,1,2,0:T(2,128)(2,1)S(1)}, u32[]{:S(2)}, u32[]{:S(2)}) async-start(bf16[48,2,7,1024]{3,1,2,0:T(2,128)(2,1)} %copy.43), calls=%async_computation.1 | async-start | bytes 2752512 | tf_op jit(solution)/shard_map/all_to_all | solution.py:48
  145.8 0.8 convert_bitcast_fusion
  146.6 63.7 %psum.7 = bf16[8,2048]{1,0:T(8,128)(2,1)S(1)} all-reduce(bf16[8,2048]{1,0:T(8,128)(2,1)S(1)} %convert_bitcast_fusion), channel_id=1, replica_groups=mesh['replica'=16,'expert'=48] {'replica'}, use_global_device_ids=true, to_apply=%region_10.11 | all-reduce | flops 16384 | bytes 65536 | tf_op jit(solution)/shard_map/psum | solution.py:68
  210.3 1.5 multiply_subtract_fusion
  211.9 0.9 copy.49
  212.7 1.1 copy.48
  213.9 2.8 %copy_dynamic-update-slice_fusion.1 = bf16[2,672,1024]{2,1,0:T(8,128)(2,1)} fusion(bf16[2,336,1024]{2,0,1:T(2,128)(2,1)} %bitcast.6), kind=kLoop, calls=%fused_computation.17 | loop fusion | bytes 2752512
  216.7 1.5 copy_dynamic-update-slice_fusion
  218.2 0.1 copy-done.6
  218.3 3.5 %fusion.30 = f32[2,672,384]{2,1,0:T(8,128)S(1)} fusion(bf16[2,672,1024]{2,1,0:T(8,128)(2,1)} %copy_dynamic-update-slice_fusion, bf16[2,1024,384]{2,1,0:T(8,128)(2,1)S(1)} %copy-done.6), kind=kOutput, calls=%fused_computation.59 | convolution fusion | flops 1056964608 | bytes 6389760 | tf_op jit(solution)/shard_map/erd,edf->erf/dot_general | solution.py:55
  221.8 1.3 copy-done.7
  223.2 3.1 %fusion.6 = bf16[1,2,1024,384]{3,2,1,0:T(8,128)(2,1)} fusion(bf16[2,672,1024]{2,1,0:T(8,128)(2,1)S(1)} %copy-done.3, f32[2,672,384]{2,1,0:T(8,128)S(1)} %fusion.30, bf16[2,336,384]{2,1,0:T(8,128)(2,1)S(1)} %copy-done.4, bf16[2,336,384]{2,1,0:T(8,128)(2,1)S(1)} %copy.48), kind=kOutput, calls=%fused_computation.15 | convolution fusion | flops 1062912000 | bytes 7421952 | tf_op jit(solution)/shard_map/erd,erf->edf/dot_general | solution.py:64
  226.2 7.7 %fusion.5 = bf16[1,2,1024,384]{3,2,1,0:T(8,128)(2,1)} fusion(bf16[2,672,1024]{2,1,0:T(8,128)(2,1)} %copy_dynamic-update-slice_fusion, f32[2,672,384]{2,1,0:T(8,128)} %copy-done.7, bf16[2,1024,384]{2,1,0:T(8,128)(2,1)S(1)} %copy-done, bf16[2,336,384]{2,1,0:T(8,128)(2,1)S(1)} %copy-done.4, bf16[2,336,384]{2,1,0:T(8,128)(2,1)S(1)} %copy.48), kind=kOutput, calls=%fused_computation.14 | convolution fusion | flops 2121940992 | bytes 8994816 | tf_op jit(solution)/shard_map/erd,erf->edf/dot_general | solution.py:61
  (18 shorter events, 0.1 us)
Async XLA Ops:
  0.6 225.6 %copy-start = (bf16[2,1024,384]{2,1,0:T(8,128)(2,1)S(1)}, bf16[2,1024,384]{2,1,0:T(8,128)(2,1)}, u32[]{:S(2)}) copy-start(bf16[2,1024,384]{2,1,0:T(8,128)(2,1)} %param.12) | copy-start | bytes 4718596
  7.7 39.3 %all-to-all-start.3 = ((bf16[48,2,7,384]{3,1,2,0:T(2,128)(2,1)}), bf16[48,2,7,384]{3,1,2,0:T(2,128)(2,1)S(1)}, u32[]{:S(2)}, u32[]{:S(2)}) async-start(bf16[48,2,7,384]{3,1,2,0:T(2,128)(2,1)} %copy.47), calls=%async_computation.3 | async-start | bytes 1032192 | tf_op jit(solution)/shard_map/all_to_all | solution.py:49
  28.1 28.8 %copy-start.5 = (bf16[1,128,1024]{2,1,0:T(8,128)(2,1)S(1)}, bf16[1,128,1024]{2,1,0:T(8,128)(2,1)}, u32[]{:S(2)}) copy-start(bf16[1,128,1024]{2,1,0:T(8,128)(2,1)} %param.8) | copy-start | bytes 786436
  47.0 9.9 %copy-start.1 = (bf16[48,2,7,384]{3,1,2,0:T(2,128)(2,1)}, bf16[48,2,7,384]{3,1,2,0:T(2,128)(2,1)S(1)}, u32[]{:S(2)}) copy-start(bf16[48,2,7,384]{3,1,2,0:T(2,128)(2,1)S(1)} %all-to-all-done.3) | copy-start | bytes 1548292
  47.0 30.7 %all-to-all-start.2 = ((bf16[48,2,7,384]{3,1,2,0:T(2,128)(2,1)}), bf16[48,2,7,384]{3,1,2,0:T(2,128)(2,1)}, u32[]{:S(2)}, u32[]{:S(2)}) async-start(bf16[48,2,7,384]{3,1,2,0:T(2,128)(2,1)} %copy.46), calls=%async_computation.2 | async-start | bytes 1032192 | tf_op jit(solution)/shard_map/all_to_all | solution.py:49
  77.7 56.1 %all-to-all-start = ((bf16[48,2,7,1024]{3,1,2,0:T(2,128)(2,1)}), bf16[48,2,7,1024]{3,1,2,0:T(2,128)(2,1)}, u32[]{:S(2)}, u32[]{:S(2)}) async-start(bf16[48,2,7,1024]{3,1,2,0:T(2,128)(2,1)} %copy.40), calls=%async_computation | async-start | bytes 2752512 | tf_op jit(solution)/shard_map/all_to_all | solution.py:48
  96.2 115.7 %copy-start.2 = (bf16[48,2,7,384]{3,1,2,0:T(2,128)(2,1)S(1)}, bf16[48,2,7,384]{3,1,2,0:T(2,128)(2,1)}, u32[]{:S(2)}) copy-start(bf16[48,2,7,384]{3,1,2,0:T(2,128)(2,1)} %copy-done.1) | copy-start | bytes 1548292
  133.8 82.9 %all-to-all-start.1 = ((bf16[48,2,7,1024]{3,1,2,0:T(2,128)(2,1)}), bf16[48,2,7,1024]{3,1,2,0:T(2,128)(2,1)S(1)}, u32[]{:S(2)}, u32[]{:S(2)}) async-start(bf16[48,2,7,1024]{3,1,2,0:T(2,128)(2,1)} %copy.43), calls=%async_computation.1 | async-start | bytes 2752512 | tf_op jit(solution)/shard_map/all_to_all | solution.py:48
  216.7 1.6 copy-start.6
  218.3 4.9 %copy-start.3 = (bf16[2,672,1024]{2,1,0:T(8,128)(2,1)S(1)}, bf16[2,672,1024]{2,1,0:T(8,128)(2,1)}, u32[]{:S(2)}) copy-start(bf16[2,672,1024]{2,1,0:T(8,128)(2,1)} %copy_dynamic-update-slice_fusion) | copy-start | bytes 8257540
  218.3 4.9 %copy-start.4 = (bf16[2,336,384]{2,1,0:T(8,128)(2,1)S(1)}, bf16[2,336,384]{2,1,0:T(8,128)(2,1)}, u32[]{:S(2)}) copy-start(bf16[2,336,384]{2,1,0:T(8,128)(2,1)} %copy.49) | copy-start | bytes 1548292
  221.8 1.3 copy-start.7
where the time goes:
time: 235 us; the launch traced here: 234 us
  waiting for transfers between devices  64.1 us (27%)
  blocking collectives  63.7 us (27%)
  starting transfers between devices  50.2 us (21%)
  local copies, waits for them, and re-layouts  34.4 us (15%)
  matrix products  14.3 us (6%)
  other arithmetic  6.3 us (3%)
    psum x1, blocking collectives, local(): lax.psum(inner_params[0].astype(jnp.bfloat16), 'replica')  63.7 us
    all_to_all x2, waiting for transfers between devices, local(): lax.all_to_all(send_x, 'expert', split_axis=0, concat_axis=2, tiled=True)  37.5 us
    all_to_all x2, starting transfers between devices, local(): lax.all_to_all(send_h, 'expert', split_axis=0, concat_axis=2, tiled=True)  28.4 us
    all_to_all x2, waiting for transfers between devices, local(): lax.all_to_all(send_h, 'expert', split_axis=0, concat_axis=2, tiled=True)  26.6 us
    all_to_all x2, starting transfers between devices, local(): lax.all_to_all(send_x, 'expert', split_axis=0, concat_axis=2, tiled=True)  21.8 us
    reshape x4, local copies, waits for them, and re-layouts, local(): send_x = send_x.reshape(groups, local_count, capacity, width)  9.9 us
    dot_general x1, matrix products, local(): jnp.einsum('erd,erf->edf', rows_x, gate_d, preferred_element_type=jnp.flo...  7.72 us
    scatter x2, local copies, waits for them, and re-layouts, local(): jnp.zeros((experts_all * capacity, width), jnp.bfloat16).at[flat]  7.44 us
  transfers between devices with their start and end apart: 4, of which 3 were waited for; matrix products, arithmetic and copies ran while one was open for 13% of the time, Pallas kernels for 0%

commit v1 on v0

v1 whole, which is shorter than its diff:
```python
import jax
import jax.numpy as jnp
from jax import lax
from jax.experimental import pallas as pl
from jax.experimental.pallas import tpu as pltpu
from jax.sharding import PartitionSpec as P

MESH = pl.DeviceIdType.MESH
NZ = 12
NY = 8
SLOTS = 7
ROWS = 16
ARRIVAL = [0, 1, 11, 2, 10, 3, 9, 4, 8, 5, 7, 6]
POS = {o: p for p, o in enumerate(ARRIVAL)}
FAR = [6, 5, 7, 4, 8, 3, 9, 2, 10, 1, 11, 0]
LEAVE = (2, 3, 4)
F32 = jnp.float32
BF16 = jnp.bfloat16


def iota(shape, dim):
    return lax.broadcasted_iota(jnp.int32, shape, dim)


def onehot(mask):
    return jnp.where(mask, 1.0, 0.0).astype(BF16)


def dispatch_kernel(
    ids_ref, tok_h, hid_h, gate_h, up_h, inner_h,
    x_o, g_o, sum_o,
    tok, meta, xs, xr, hid, hs, hq, hr, w, gu, gd, yr, part,
    load_sem, tok_s, tok_r, meta_s, meta_r, x_s, x_r, hp_s, hp_r, hz_s, hz_r,
    y_s, y_r, l_s, l_r, own_sem, out_sem,
):
    replica = lax.axis_index("replica")
    expert = lax.axis_index("expert")
    xlo, y = replica // NY, replica % NY
    xhi, z, c = expert // (2 * NZ), (expert // 2) % NZ, expert % 2

    def at(dz=0, s=0):
        x2 = (xhi + s // 2) % 2
        c2 = (c + s % 2) % 2
        return (replica, (x2 * NZ + (z + dz) % NZ) * 2 + c2)

    def at_y(dy, dl=0):
        return (((xlo + dl) % 2) * NY + (y + dy) % NY, expert)

    loads = [
        pltpu.make_async_copy(tok_h, tok.at[0], load_sem.at[0]),
        pltpu.make_async_copy(hid_h, hid, load_sem.at[1]),
        pltpu.make_async_copy(gate_h, w.at[:, :, pl.ds(0, 384)], load_sem.at[2]),
        pltpu.make_async_copy(up_h, w.at[:, :, pl.ds(384, 384)], load_sem.at[3]),
        pltpu.make_async_copy(inner_h, yr.at[y], load_sem.at[4]),
    ]
    for load in loads:
        load.start()

    barrier = pltpu.get_barrier_semaphore()
    peers = [at(dz) for dz in range(1, NZ)] + [at(0, s) for s in (1, 2, 3)]
    peers += [at_y(dy) for dy in range(1, NY)] + [at_y(0, 1)]
    for peer in peers:
        pl.semaphore_signal(barrier, inc=1, device_id=peer, device_id_type=MESH)
    pl.semaphore_wait(barrier, len(peers))

    def remote(src, dst, send, recv, device):
        return pltpu.make_async_remote_copy(
            src_ref=src, dst_ref=dst, send_sem=send, recv_sem=recv,
            device_id=device, device_id_type=MESH,
        )

    def token_copy(step, way, half):
        sign = 1 if way == 0 else -1
        rows = pl.ds(half * 64, 64)
        dst = POS[(sign * step) % NZ]
        src = tok_h.at[rows] if step == 1 else tok.at[POS[(sign * (step - 1)) % NZ], rows]
        return remote(
            src, tok.at[dst, rows], tok_s.at[dst, half], tok_r.at[dst, half], at(-sign)
        )

    def meta_copy(step, way):
        sign = 1 if way == 0 else -1
        dst = POS[(sign * step) % NZ]
        return remote(
            meta.at[POS[(sign * (step - 1)) % NZ]], meta.at[dst],
            meta_s.at[dst], meta_r.at[dst], at(-sign),
        )

    def ways(step, half):
        return (0, 1) if step < NZ // 2 else (half,)

    sent = []

    def go(copy):
        copy.start()
        sent.append(copy)
        return copy

    ring = {}
    for half in (0, 1):
        for way in ways(1, half):
            ring[1, way, half] = go(token_copy(1, way, half))
    gathers = [
        go(remote(inner_h, yr.at[y], y_s.at[dy], y_r.at[dy], at_y(dy))) for dy in range(1, NY)
    ]

    pick = onehot(iota((128, 1024), 1) // 8 == iota((128, 1024), 0))
    spread = jnp.dot(ids_ref[...].astype(F32).astype(BF16), pick, preferred_element_type=F32)
    mine = iota((8, 1024), 1) % 8 == iota((8, 1024), 0)
    ids = jnp.sum(jnp.where(mine, spread, 0.0), axis=0, keepdims=True)
    earlier = onehot(iota((512, 512), 0) // 8 < iota((512, 512), 1) // 8)
    experts = iota((96, 512), 0).astype(F32)
    slots = []
    for block in (0, 1):
        hits = experts == ids[:, block * 512 : (block + 1) * 512]
        before = jnp.dot(onehot(hits), earlier, preferred_element_type=F32)
        slots.append(
            jnp.sum(jnp.where(hits, before, 0.0), axis=0, keepdims=True) + float(SLOTS * block)
        )
    slot = jnp.concatenate(slots, axis=1)
    chip = jnp.floor(ids * 0.25)
    far_x = jnp.where(chip >= float(NZ), 1.0, 0.0)
    inside = ids - 4.0 * chip
    core = jnp.where(inside >= 2.0, 1.0, 0.0)
    local = inside - 2.0 * core
    dz = chip - float(NZ) * far_x - z.astype(F32)
    dz = jnp.where(dz < 0.0, dz + float(NZ), dz)
    rel = jnp.where(far_x == xhi.astype(F32), 0.0, 2.0) + jnp.where(core == c.astype(F32), 0.0, 1.0)
    lane = rel * 32.0 + local * 16.0 + slot
    order = jnp.where(
        dz > 6.0, 2.0 * dz - 12.0, jnp.where(dz == 6.0, 0.0, 11.0 - 2.0 * dz)
    )
    row = order * 128.0 + lane
    token = (iota((16, 1024), 1) // 8 + 1).astype(F32)
    lines = jnp.where(iota((16, 1024), 0).astype(F32) == dz, token, 0.0).astype(BF16)
    places = onehot(iota((128, 1024), 0).astype(F32) == lane)
    meta[0] = lax.dot_general(
        lines, places, (((1,), (1,)), ((), ())), preferred_element_type=F32
    )
    metas = {}
    for way in (0, 1):
        metas[1, way] = go(meta_copy(1, way))

    loads[1].wait()
    plane = {}
    rows_of = iota((256, 1024), 0).astype(F32)
    for third in range(3):
        for pair in (2 * third, 2 * third + 1):
            take = onehot(rows_of == row - float(256 * pair))
            packed = jnp.dot(take, hid[...], preferred_element_type=F32).astype(BF16)
            for i in range(2):
                for s in range(4):
                    for e in range(2):
                        at_row = ((i * 4 + s) * 2 + e) * ROWS
                        hs[2 * pair + i, s, e] = packed[at_row : at_row + ROWS]
        part_of = pl.ds(4 * third, 4)
        for s in (1, 2, 3):
            plane[third, s] = go(
                remote(
                    hs.at[part_of, s], hq.at[part_of, s],
                    hp_s.at[third, s], hp_r.at[third, s], at(0, s),
                )
            )
        plane[third, 0] = pltpu.make_async_copy(
            hs.at[part_of, 0], hq.at[part_of, 0], hp_r.at[third, 0]
        )
        plane[third, 0].start()

    rows_sent = {}

    def pick_rows(offset):
        p = POS[offset]
        line = (-offset) % NZ
        wanted = meta[p][line : line + 1, :]
        take = onehot((iota((128, 128), 0) + 1).astype(F32) == wanted)
        rows = lax.dot_general(
            take, tok[p], (((0,), (0,)), ((), ())), preferred_element_type=F32
        ).astype(BF16)
        for s in range(4):
            for e in range(2):
                at_row = (s * 2 + e) * ROWS
                xs[p, s, e] = rows[at_row : at_row + ROWS]
        for s in (1, 2, 3):
            rows_sent[p, s] = go(
                remote(xs.at[p, s], xr.at[p, s], x_s.at[p, s], x_r.at[p, s], at(0, s))
            )
        rows_sent[p, 0] = pltpu.make_async_copy(xs.at[p, 0], xr.at[p, 0], x_r.at[p, 0])
        rows_sent[p, 0].start()

    stay = pltpu.make_async_copy(hq.at[11], hr.at[POS[0]], own_sem.at[0])
    along = {}

    def leave(third):
        plane[third, 0].wait()
        for s in (1, 2, 3):
            plane[third, s].wait_recv()
        for q in range(4 * third, 4 * third + 4):
            distance = FAR[q]
            if distance == 0:
                stay.start()
            else:
                p = POS[(-distance) % NZ]
                along[p] = go(
                    remote(hq.at[q], hr.at[p], hz_s.at[p], hz_r.at[p], at(distance))
                )

    outs = []

    def project(group):
        for p in range(4 * group, 4 * group + 4):
            rows_sent[p, 0].wait()
            for s in (1, 2, 3):
                rows_sent[p, s].wait_recv()
        for e in range(2):
            block = pl.ds(4 * group, 4)
            rows = xr[block, :, e].reshape(256, 1024)
            gu[e, group] = jnp.dot(rows, w[e], preferred_element_type=F32)
            out = pltpu.make_async_copy(
                xr.at[block, :, e], x_o.at[e, block], out_sem.at[e, group]
            )
            out.start()
            outs.append(out)

    loads[0].wait()
    pick_rows(0)
    for step in range(1, NZ // 2 + 1):
        for half in (0, 1):
            for way in ways(step, half):
                ring[step, way, half].wait_recv()
                if step < NZ // 2 and way in ways(step + 1, half):
                    ring[step + 1, way, half] = go(token_copy(step + 1, way, half))
            if half == 0:
                for way in ways(step, 0):
                    metas[step, way].wait_recv()
                    if step < NZ // 2 and way in ways(step + 1, 0):
                        metas[step + 1, way] = go(meta_copy(step + 1, way))
        for third in range(3):
            if LEAVE[third] == step:
                leave(third)
        for offset in dict.fromkeys((step, NZ - step)):
            pick_rows(offset)
        if step == 3:
            loads[4].wait()
            for gather in gathers:
                gather.wait_recv()
            total = yr[0]
            for i in range(1, NY):
                total = total + yr[i]
            part[0] = total
            swap = go(remote(part.at[0], part.at[1], l_s, l_r, at_y(0, 1)))
        if step == 4:
            loads[2].wait()
            loads[3].wait()
            project(0)
        if step == 5:
            swap.wait_recv()
            sum_o[...] = part[0] + part[1]
        if step == 6:
            project(1)
    project(2)

    stay_waited = False
    for group in (2, 1, 0):
        for p in range(4 * group, 4 * group + 4):
            if p == POS[0]:
                stay.wait()
            else:
                along[p].wait_recv()
        for e in range(2):
            cot = hr[pl.ds(4 * group, 4), :, e].reshape(256, 384).astype(F32)
            gate = gu[e, group, :, 0:384]
            up = gu[e, group, :, 384:768]
            sig = jax.nn.sigmoid(gate)
            gd[e, group, :, 0:384] = (cot * up * sig * (1.0 + gate * (1.0 - sig))).astype(BF16)
            gd[e, group, :, 384:768] = (cot * gate * sig).astype(BF16)
            out = pltpu.make_async_copy(
                gd.at[e, group], g_o.at[e, group], out_sem.at[2 + e, group]
            )
            out.start()
            outs.append(out)
    for copy in sent:
        copy.wait_send()
    for out in outs:
        out.wait()


def grad_kernel(x_ref, g_ref, sum_ref, outer_ref, mom_ref, gate_ref, up_ref, no_ref, nm_ref):
    grads = lax.dot_general(
        x_ref[0], g_ref[0], (((0,), (0,)), ((), ())), preferred_element_type=F32
    ).astype(BF16)
    gate_ref[0] = grads[:, 0:384]
    up_ref[0] = grads[:, 384:768]
    delta = outer_ref[...] - sum_ref[...] / 16.0
    momentum = 0.9 * mom_ref[...] + delta
    nm_ref[...] = momentum
    no_ref[...] = outer_ref[...] - 0.7 * (delta + 0.9 * momentum)


def local(tokens, ids, hidden, gate_weight, up_weight, outer, momentum, inner):
    any_ = pl.BlockSpec(memory_space=pl.ANY)
    vmem = pl.BlockSpec(memory_space=pltpu.VMEM)
    dma = pltpu.SemaphoreType.DMA
    x_rows, g_rows, summed = pl.pallas_call(
        dispatch_kernel,
        out_shape=(
            jax.ShapeDtypeStruct((2, NZ, 4, ROWS, 1024), BF16),
            jax.ShapeDtypeStruct((2, 3, 256, 768), BF16),
            jax.ShapeDtypeStruct((8, 2048), F32),
        ),
        in_specs=[vmem, any_, any_, any_, any_, any_],
        out_specs=(any_, any_, vmem),
        scratch_shapes=[
            pltpu.VMEM((NZ, 128, 1024), BF16),
            pltpu.VMEM((NZ, 16, 128), F32),
            pltpu.VMEM((NZ, 4, 2, ROWS, 1024), BF16),
            pltpu.VMEM((NZ, 4, 2, ROWS, 1024), BF16),
            pltpu.VMEM((1024, 384), BF16),
            pltpu.VMEM((NZ, 4, 2, ROWS, 384), BF16),
            pltpu.VMEM((NZ, 4, 2, ROWS, 384), BF16),
            pltpu.VMEM((NZ, 4, 2, ROWS, 384), BF16),
            pltpu.VMEM((2, 1024, 768), BF16),
            pltpu.VMEM((2, 3, 256, 768), F32),
            pltpu.VMEM((2, 3, 256, 768), BF16),
            pltpu.VMEM((NY, 8, 2048), F32),
            pltpu.VMEM((2, 8, 2048), F32),
            dma((5,)), dma((NZ, 2)), dma((NZ, 2)), dma((NZ,)), dma((NZ,)),
            dma((NZ, 4)), dma((NZ, 4)), dma((3, 4)), dma((3, 4)), dma((NZ,)), dma((NZ,)),
            dma((NY,)), dma((NY,)), dma, dma, dma((1,)), dma((4, 3)),
        ],
        compiler_params=pltpu.CompilerParams(
            collective_id=0, has_side_effects=True, vmem_limit_bytes=60 << 20
        ),
        cost_estimate=pl.CostEstimate(
            flops=4_000_000_000, bytes_accessed=16_000_000, transcendentals=600_000
        ),
    )(ids[0].T, tokens[0], hidden[0].reshape(1024, 384), gate_weight, up_weight, inner[0])
    x_rows = x_rows.reshape(2, 768, 1024)
    g_rows = g_rows.reshape(2, 768, 768)
    gate_grad, up_grad, new_outer, new_momentum = pl.pallas_call(
        grad_kernel,
        grid=(2, 2),
        out_shape=(
            jax.ShapeDtypeStruct((2, 1024, 384), BF16),
            jax.ShapeDtypeStruct((2, 1024, 384), BF16),
            jax.ShapeDtypeStruct((8, 2048), F32),
            jax.ShapeDtypeStruct((8, 2048), F32),
        ),
        in_specs=[
            pl.BlockSpec((1, 768, 512), lambda e, m: (e, 0, m)),
            pl.BlockSpec((1, 768, 768), lambda e, m: (e, 0, 0)),
            pl.BlockSpec((8, 2048), lambda e, m: (0, 0)),
            pl.BlockSpec((8, 2048), lambda e, m: (0, 0)),
            pl.BlockSpec((8, 2048), lambda e, m: (0, 0)),
        ],
        out_specs=(
            pl.BlockSpec((1, 512, 384), lambda e, m: (e, m, 0)),
            pl.BlockSpec((1, 512, 384), lambda e, m: (e, m, 0)),
            pl.BlockSpec((8, 2048), lambda e, m: (0, 0)),
            pl.BlockSpec((8, 2048), lambda e, m: (0, 0)),
        ),
        compiler_params=pltpu.CompilerParams(vmem_limit_bytes=60 << 20),
    )(x_rows, g_rows, summed, outer, momentum)
    return gate_grad[None], up_grad[None], new_outer, new_momentum


def solution(mesh):
    rows = P("replica", "expert", None)
    return jax.shard_map(
        local,
        mesh=mesh,
        in_specs=(
            rows,
            rows,
            P("replica", "expert", None, None),
            P("expert", None, None),
            P("expert", None, None),
            P("expert", None),
            P("expert", None),
            rows,
        ),
        out_specs=(
            P("replica", "expert", None, None),
            P("replica", "expert", None, None),
            P("expert", None),
            P("expert", None),
        ),
        check_vma=False,
    )
```

time: 235 us -> 111 us (0.47)
  the two profiles are of different devices: /device:TPU:6 before, /device:TPU:1 now
where the time goes in v1:
time: 111 us
  Pallas kernels  111 us (100%)
    pallas_call x1, Pallas kernels, local(): pl.pallas_call(dispatch_kernel, out_shape=(jax.ShapeDtypeStruct((2, NZ, 4...  104 us
    pallas_call x1, Pallas kernels, local(): pl.pallas_call(grad_kernel, grid=(2, 2), out_shape=(jax.ShapeDtypeStruct(...  6.79 us

profile of v1, /device:TPU:1, one launch (start us, length us, event | category | flops | bytes accessed | tf_op | source)
XLA Modules:
  0.0 111.2 jit_solution(3060122927068043217)
XLA Ops:
  0.6 103.8 %shard_map.111 = (bf16[2,12,4,16,1024]{4,3,2,1,0:T(8,128)(2,1)}, bf16[2,3,256,768]{3,2,1,0:T(8,128)(2,1)}, f32[8,2048]{1,0:T(8,128)}) custom-call(s32[8,128]{1,0:T(8,128)} %bitcast.17, bf16[128,1024]{1,0:T(8,128)(2,1)} %bitcast.15, bf16[1024,384]{1,0:T(8,128)(2,1)} %bitcast.14, bf16[2,1024,384]{2,1,0:T(8,128)(2,1)} %gate_h.1, bf16[2,1024,384]{2,1,0:T(8,128)(2,1)} %up_h.1, ...), custom_call_target="tpu_custom_call" | custom-call | flops 4000000000 | bytes 16000000 | tf_op jit(solution)/shard_map/pallas_call | solution.py:303
  104.4 6.8 %shard_map.112 = (bf16[2,1024,384]{2,1,0:T(8,128)(2,1)}, bf16[2,1024,384]{2,1,0:T(8,128)(2,1)}, f32[8,2048]{1,0:T(8,128)}, f32[8,2048]{1,0:T(8,128)}) custom-call(bf16[2,768,1024]{2,1,0:T(8,128)(2,1)} %bitcast.10, bf16[2,768,768]{2,1,0:T(8,128)(2,1)} %bitcast.11, f32[8,2048]{1,0:T(8,128)} %get-tuple-element.13.sum_ref, f32[8,2048]{1,0:T(8,128)} %outer_ref.1, ...), custom_call_target="tpu_custom_call" | custom-call | tf_op jit(solution)/shard_map/pallas_call | solution.py:339

commit v2 on v1

--- a/solution.py
+++ b/solution.py
@@ -13,7 +13,10 @@
 ARRIVAL = [0, 1, 11, 2, 10, 3, 9, 4, 8, 5, 7, 6]
 POS = {o: p for p, o in enumerate(ARRIVAL)}
 FAR = [6, 5, 7, 4, 8, 3, 9, 2, 10, 1, 11, 0]
-LEAVE = (2, 3, 4)
+LEAVE = (4, 4, 5, 5, 5, 5, 5, 6, 6, 6, 6, 6)
+FINISH = (2, 1, 0)
+PAIR = 28
+LINE = 4 * PAIR
 F32 = jnp.float32
 BF16 = jnp.bfloat16
 
@@ -26,12 +29,21 @@
     return jnp.where(mask, 1.0, 0.0).astype(BF16)
 
 
+def digits(value, *weights):
+    out = []
+    for weight in weights:
+        digit = jnp.floor((value + 0.5) * (1.0 / weight))
+        value = value - digit * weight
+        out.append(digit)
+    return (*out, value)
+
+
 def dispatch_kernel(
     ids_ref, tok_h, hid_h, gate_h, up_h, inner_h,
-    x_o, g_o, sum_o,
-    tok, meta, xs, xr, hid, hs, hq, hr, w, gu, gd, yr, part,
+    x_o, g_o, some_o, sum_o,
+    tok, meta, xs, xr, xt, hid, hs, hq, hz, hr, w, gu, gd, acc, some, yr, part,
     load_sem, tok_s, tok_r, meta_s, meta_r, x_s, x_r, hp_s, hp_r, hz_s, hz_r,
-    y_s, y_r, l_s, l_r, own_sem, out_sem,
+    y_s, y_r, l_s, l_r, out_sem,
 ):
     replica = lax.axis_index("replica")
     expert = lax.axis_index("expert")
@@ -127,10 +139,12 @@
     dz = jnp.where(dz < 0.0, dz + float(NZ), dz)
     rel = jnp.where(far_x == xhi.astype(F32), 0.0, 2.0) + jnp.where(core == c.astype(F32), 0.0, 1.0)
     lane = rel * 32.0 + local * 16.0 + slot
-    order = jnp.where(
-        dz > 6.0, 2.0 * dz - 12.0, jnp.where(dz == 6.0, 0.0, 11.0 - 2.0 * dz)
-    )
-    row = order * 128.0 + lane
+    order = jnp.zeros_like(dz)
+    for q, distance in enumerate(FAR):
+        order = order + jnp.where(dz == float(distance), float(q), 0.0)
+    third_of = jnp.floor(order * 0.25)
+    row = third_of * (4.0 * LINE) + rel * float(LINE) + (order - 4.0 * third_of) * float(PAIR)
+    row = row + local * 14.0 + slot
     token = (iota((16, 1024), 1) // 8 + 1).astype(F32)
     lines = jnp.where(iota((16, 1024), 0).astype(F32) == dz, token, 0.0).astype(BF16)
     places = onehot(iota((128, 1024), 0).astype(F32) == lane)
@@ -143,28 +157,20 @@
 
     loads[1].wait()
     plane = {}
-    rows_of = iota((256, 1024), 0).astype(F32)
+    rows_of = iota((4 * LINE, 1024), 0).astype(F32)
     for third in range(3):
-        for pair in (2 * third, 2 * third + 1):
-            take = onehot(rows_of == row - float(256 * pair))
-            packed = jnp.dot(take, hid[...], preferred_element_type=F32).astype(BF16)
-            for i in range(2):
-                for s in range(4):
-                    for e in range(2):
-                        at_row = ((i * 4 + s) * 2 + e) * ROWS
-                        hs[2 * pair + i, s, e] = packed[at_row : at_row + ROWS]
-        part_of = pl.ds(4 * third, 4)
+        take = onehot(rows_of == row - float(4 * LINE * third))
+        packed = jnp.dot(take, hid[...], preferred_element_type=F32).astype(BF16)
+        hs[third] = packed
         for s in (1, 2, 3):
+            piece = pl.ds(s * LINE, LINE)
             plane[third, s] = go(
                 remote(
-                    hs.at[part_of, s], hq.at[part_of, s],
+                    hs.at[third, piece], hq.at[third, piece],
                     hp_s.at[third, s], hp_r.at[third, s], at(0, s),
                 )
             )
-        plane[third, 0] = pltpu.make_async_copy(
-            hs.at[part_of, 0], hq.at[part_of, 0], hp_r.at[third, 0]
-        )
-        plane[third, 0].start()
+        hq[third, 0:LINE] = packed[0:LINE]
 
     rows_sent = {}
 
@@ -187,22 +193,31 @@
         rows_sent[p, 0] = pltpu.make_async_copy(xs.at[p, 0], xr.at[p, 0], x_r.at[p, 0])
         rows_sent[p, 0].start()
 
-    stay = pltpu.make_async_copy(hq.at[11], hr.at[POS[0]], own_sem.at[0])
     along = {}
-
-    def leave(third):
-        plane[third, 0].wait()
+    column = iota((1, 4 * LINE), 1).astype(F32)
+    sender, receiver, rest = digits(column, LINE, PAIR)
+    turned = onehot(
+        iota((4 * LINE, 4 * LINE), 0).astype(F32) == receiver * LINE + sender * PAIR + rest
+    )
+
+    def turn(third):
         for s in (1, 2, 3):
             plane[third, s].wait_recv()
-        for q in range(4 * third, 4 * third + 4):
-            distance = FAR[q]
-            if distance == 0:
-                stay.start()
-            else:
-                p = POS[(-distance) % NZ]
-                along[p] = go(
-                    remote(hq.at[q], hr.at[p], hz_s.at[p], hz_r.at[p], at(distance))
-                )
+        lines = jnp.dot(turned, hq[third], preferred_element_type=F32).astype(BF16)
+        hz[third] = lines
+        for i in range(4):
+            if FAR[4 * third + i] == 0:
+                hr[0, 0:LINE] = lines[i * LINE : (i + 1) * LINE]
+
+    def leave(q):
+        p = POS[(-FAR[q]) % NZ]
+        along[p] = go(
+            remote(
+                hz.at[q // 4, pl.ds(q % 4 * LINE, LINE)],
+                hr.at[p // 4, pl.ds(p % 4 * LINE, LINE)],
+                hz_s.at[p], hz_r.at[p], at(FAR[q]),
+            )
+        )
 
     outs = []
 
@@ -214,12 +229,14 @@
         for e in range(2):
             block = pl.ds(4 * group, 4)
             rows = xr[block, :, e].reshape(256, 1024)
+            xt[e, :, 256 * group : 256 * group + 256] = rows.T
             gu[e, group] = jnp.dot(rows, w[e], preferred_element_type=F32)
-            out = pltpu.make_async_copy(
-                xr.at[block, :, e], x_o.at[e, block], out_sem.at[e, group]
-            )
-            out.start()
-            outs.append(out)
+            if group == FINISH[2]:
+                out = pltpu.make_async_copy(
+                    xt.at[e, :, pl.ds(256 * group, 256)], x_o.at[e], out_sem.at[0, e]
+                )
+                out.start()
+                outs.append(out)
 
     loads[0].wait()
     pick_rows(0)
@@ -235,8 +252,11 @@
                     if step < NZ // 2 and way in ways(step + 1, 0):
                         metas[step + 1, way] = go(meta_copy(step + 1, way))
         for third in range(3):
-            if LEAVE[third] == step:
-                leave(third)
+            if min(LEAVE[4 * third : 4 * third + 4]) == step:
+                turn(third)
+        for q in range(NZ):
+            if LEAVE[q] == step and FAR[q] != 0:
+                leave(q)
         for offset in dict.fromkeys((step, NZ - step)):
             pick_rows(offset)
         if step == 3:
@@ -259,35 +279,50 @@
             project(1)
     project(2)
 
-    stay_waited = False
-    for group in (2, 1, 0):
+    at_p, at_s, at_e, at_slot = digits(column, LINE, PAIR, 14)
+    target = iota((256, 4 * LINE), 0).astype(F32)
+    goal = (at_p * 4.0 + at_s) * float(ROWS) + at_slot
+    spaced = [onehot((target == goal) & (at_e == float(e))) for e in range(2)]
+    for group in FINISH:
         for p in range(4 * group, 4 * group + 4):
-            if p == POS[0]:
-                stay.wait()
-            else:
+            if p in along:
                 along[p].wait_recv()
         for e in range(2):
-            cot = hr[pl.ds(4 * group, 4), :, e].reshape(256, 384).astype(F32)
+            cot = jnp.dot(spaced[e], hr[group], preferred_element_type=F32)
             gate = gu[e, group, :, 0:384]
             up = gu[e, group, :, 384:768]
             sig = jax.nn.sigmoid(gate)
             gd[e, group, :, 0:384] = (cot * up * sig * (1.0 + gate * (1.0 - sig))).astype(BF16)
             gd[e, group, :, 384:768] = (cot * gate * sig).astype(BF16)
-            out = pltpu.make_async_copy(
-                gd.at[e, group], g_o.at[e, group], out_sem.at[2 + e, group]
-            )
-            out.start()
-            outs.append(out)
+            if group == FINISH[2]:
+                out = pltpu.make_async_copy(gd.at[e, group], g_o.at[e], out_sem.at[1, e])
+                out.start()
+                outs.append(out)
+                continue
+            for m in range(4):
+                rows = slice(256 * m, 256 * m + 256)
+                grads = jnp.dot(
+                    xt[e, rows, 256 * group : 256 * group + 256],
+                    gd[e, group],
+                    preferred_element_type=F32,
+                )
+                if group == FINISH[0]:
+                    acc[e, rows] = grads
+                else:
+                    some[e, rows] = (acc[e, rows] + grads).astype(BF16)
+            if group == FINISH[1]:
+                out = pltpu.make_async_copy(some.at[e], some_o.at[e], out_sem.at[2, e])
+                out.start()
+                outs.append(out)
     for copy in sent:
         copy.wait_send()
     for out in outs:
         out.wait()
 
 
-def grad_kernel(x_ref, g_ref, sum_ref, outer_ref, mom_ref, gate_ref, up_ref, no_ref, nm_ref):
-    grads = lax.dot_general(
-        x_ref[0], g_ref[0], (((0,), (0,)), ((), ())), preferred_element_type=F32
-    ).astype(BF16)
+def grad_kernel(x_ref, g_ref, some_ref, sum_ref, outer_ref, mom_ref, gate_ref, up_ref, no_ref, nm_ref):
+    grads = jnp.dot(x_ref[0], g_ref[0], preferred_element_type=F32)
+    grads = (grads + some_ref[0].astype(F32)).astype(BF16)
     gate_ref[0] = grads[:, 0:384]
     up_ref[0] = grads[:, 384:768]
     delta = outer_ref[...] - sum_ref[...] / 16.0
@@ -300,32 +335,37 @@
     any_ = pl.BlockSpec(memory_space=pl.ANY)
     vmem = pl.BlockSpec(memory_space=pltpu.VMEM)
     dma = pltpu.SemaphoreType.DMA
-    x_rows, g_rows, summed = pl.pallas_call(
+    x_rows, g_rows, some, summed = pl.pallas_call(
         dispatch_kernel,
         out_shape=(
-            jax.ShapeDtypeStruct((2, NZ, 4, ROWS, 1024), BF16),
-            jax.ShapeDtypeStruct((2, 3, 256, 768), BF16),
+            jax.ShapeDtypeStruct((2, 1024, 256), BF16),
+            jax.ShapeDtypeStruct((2, 256, 768), BF16),
+            jax.ShapeDtypeStruct((2, 1024, 768), BF16),
             jax.ShapeDtypeStruct((8, 2048), F32),
         ),
         in_specs=[vmem, any_, any_, any_, any_, any_],
-        out_specs=(any_, any_, vmem),
+        out_specs=(any_, any_, any_, vmem),
         scratch_shapes=[
             pltpu.VMEM((NZ, 128, 1024), BF16),
             pltpu.VMEM((NZ, 16, 128), F32),
             pltpu.VMEM((NZ, 4, 2, ROWS, 1024), BF16),
             pltpu.VMEM((NZ, 4, 2, ROWS, 1024), BF16),
+            pltpu.VMEM((2, 1024, 768), BF16),
             pltpu.VMEM((1024, 384), BF16),
-            pltpu.VMEM((NZ, 4, 2, ROWS, 384), BF16),
-            pltpu.VMEM((NZ, 4, 2, ROWS, 384), BF16),
-            pltpu.VMEM((NZ, 4, 2, ROWS, 384), BF16),
+            pltpu.VMEM((3, 4 * LINE, 384), BF16),
+            pltpu.VMEM((3, 4 * LINE, 384), BF16),
+            pltpu.VMEM((3, 4 * LINE, 384), BF16),
+            pltpu.VMEM((3, 4 * LINE, 384), BF16),
             pltpu.VMEM((2, 1024, 768), BF16),
             pltpu.VMEM((2, 3, 256, 768), F32),
             pltpu.VMEM((2, 3, 256, 768), BF16),
+            pltpu.VMEM((2, 1024, 768), F32),
+            pltpu.VMEM((2, 1024, 768), BF16),
             pltpu.VMEM((NY, 8, 2048), F32),
             pltpu.VMEM((2, 8, 2048), F32),
             dma((5,)), dma((NZ, 2)), dma((NZ, 2)), dma((NZ,)), dma((NZ,)),
             dma((NZ, 4)), dma((NZ, 4)), dma((3, 4)), dma((3, 4)), dma((NZ,)), dma((NZ,)),
-            dma((NY,)), dma((NY,)), dma, dma, dma((1,)), dma((4, 3)),
+            dma((NY,)), dma((NY,)), dma, dma, dma((3, 2)),
         ],
         compiler_params=pltpu.CompilerParams(
             collective_id=0, has_side_effects=True, vmem_limit_bytes=60 << 20
@@ -334,8 +374,6 @@
             flops=4_000_000_000, bytes_accessed=16_000_000, transcendentals=600_000
         ),
     )(ids[0].T, tokens[0], hidden[0].reshape(1024, 384), gate_weight, up_weight, inner[0])
-    x_rows = x_rows.reshape(2, 768, 1024)
-    g_rows = g_rows.reshape(2, 768, 768)
     gate_grad, up_grad, new_outer, new_momentum = pl.pallas_call(
         grad_kernel,
         grid=(2, 2),
@@ -346,8 +384,9 @@
             jax.ShapeDtypeStruct((8, 2048), F32),
         ),
         in_specs=[
-            pl.BlockSpec((1, 768, 512), lambda e, m: (e, 0, m)),
-            pl.BlockSpec((1, 768, 768), lambda e, m: (e, 0, 0)),
+            pl.BlockSpec((1, 512, 256), lambda e, m: (e, m, 0)),
+            pl.BlockSpec((1, 256, 768), lambda e, m: (e, 0, 0)),
+            pl.BlockSpec((1, 512, 768), lambda e, m: (e, m, 0)),
             pl.BlockSpec((8, 2048), lambda e, m: (0, 0)),
             pl.BlockSpec((8, 2048), lambda e, m: (0, 0)),
             pl.BlockSpec((8, 2048), lambda e, m: (0, 0)),
@@ -359,7 +398,7 @@
             pl.BlockSpec((8, 2048), lambda e, m: (0, 0)),
         ),
         compiler_params=pltpu.CompilerParams(vmem_limit_bytes=60 << 20),
-    )(x_rows, g_rows, summed, outer, momentum)
+    )(x_rows, g_rows, some, summed, outer, momentum)
     return gate_grad[None], up_grad[None], new_outer, new_momentum
 
 

time: 111 us -> 96.8 us (0.87); the launches traced: 111 us -> 95.2 us
  Pallas kernels: 111 us -> 94.6 us
    pallas_call x1, Pallas kernels: 104 us -> 89.2 us  [local(): pl.pallas_call(dispatch_kernel, out_shape=(jax.ShapeDtypeStruct((2, 1024,...]
    pallas_call x1, Pallas kernels: 6.79 us -> 5.33 us  [local(): pl.pallas_call(grad_kernel, grid=(2, 2), out_shape=(jax.ShapeDtypeStruct(...]
where the time goes in v2:
time: 96.8 us; the launch traced here: 95.2 us
  Pallas kernels  94.6 us (98%)
    pallas_call x1, Pallas kernels, local(): pl.pallas_call(dispatch_kernel, out_shape=(jax.ShapeDtypeStruct((2, 1024,...  89.2 us
    pallas_call x1, Pallas kernels, local(): pl.pallas_call(grad_kernel, grid=(2, 2), out_shape=(jax.ShapeDtypeStruct(...  5.33 us

profile of v2, /device:TPU:1, one launch (start us, length us, event | category | flops | bytes accessed | tf_op | source)
XLA Modules:
  0.0 95.2 jit_solution(15505394962114479960)
XLA Ops:
  0.6 89.2 %shard_map.111 = (bf16[2,1024,256]{2,1,0:T(8,128)(2,1)}, bf16[2,256,768]{2,1,0:T(8,128)(2,1)}, bf16[2,1024,768]{2,1,0:T(8,128)(2,1)}, f32[8,2048]{1,0:T(8,128)}) custom-call(s32[8,128]{1,0:T(8,128)} %bitcast.13, bf16[128,1024]{1,0:T(8,128)(2,1)} %bitcast.11, bf16[1024,384]{1,0:T(8,128)(2,1)} %bitcast.10, bf16[2,1024,384]{2,1,0:T(8,128)(2,1)} %gate_h.1, ...), custom_call_target="tpu_custom_call" | custom-call | flops 4000000000 | bytes 16000000 | tf_op jit(solution)/shard_map/pallas_call | solution.py:338
  89.9 5.3 %shard_map.112 = (bf16[2,1024,384]{2,1,0:T(8,128)(2,1)}, bf16[2,1024,384]{2,1,0:T(8,128)(2,1)}, f32[8,2048]{1,0:T(8,128)}, f32[8,2048]{1,0:T(8,128)}) custom-call(bf16[2,1024,256]{2,1,0:T(8,128)(2,1)} %get-tuple-element.12.x_ref, bf16[2,256,768]{2,1,0:T(8,128)(2,1)} %get-tuple-element.13.g_ref, bf16[2,1024,768]{2,1,0:T(8,128)(2,1)} %get-tuple-element.14.some_ref, ...), custom_call_target="tpu_custom_call" | custom-call | tf_op jit(solution)/shard_map/pallas_call | solution.py:377

commit v3 on v2

--- a/solution.py
+++ b/solution.py
@@ -17,6 +17,8 @@
 FINISH = (2, 1, 0)
 PAIR = 28
 LINE = 4 * PAIR
+PIECES = 2
+TILES = 1
 F32 = jnp.float32
 BF16 = jnp.bfloat16
 
@@ -81,13 +83,13 @@
             device_id=device, device_id_type=MESH,
         )
 
-    def token_copy(step, way, half):
+    def token_copy(step, way, piece_no):
         sign = 1 if way == 0 else -1
-        rows = pl.ds(half * 64, 64)
+        rows = pl.ds(piece_no * (128 // PIECES), 128 // PIECES)
         dst = POS[(sign * step) % NZ]
         src = tok_h.at[rows] if step == 1 else tok.at[POS[(sign * (step - 1)) % NZ], rows]
         return remote(
-            src, tok.at[dst, rows], tok_s.at[dst, half], tok_r.at[dst, half], at(-sign)
+            src, tok.at[dst, rows], tok_s.at[dst, piece_no], tok_r.at[dst, piece_no], at(-sign)
         )
 
     def meta_copy(step, way):
@@ -98,8 +100,8 @@
             meta_s.at[dst], meta_r.at[dst], at(-sign),
         )
 
-    def ways(step, half):
-        return (0, 1) if step < NZ // 2 else (half,)
+    def ways(step, piece_no):
+        return (0, 1) if step < NZ // 2 else (piece_no // (PIECES // 2),)
 
     sent = []
 
@@ -109,9 +111,9 @@
         return copy
 
     ring = {}
-    for half in (0, 1):
-        for way in ways(1, half):
-            ring[1, way, half] = go(token_copy(1, way, half))
+    for piece_no in range(PIECES):
+        for way in ways(1, piece_no):
+            ring[1, way, piece_no] = go(token_copy(1, way, piece_no))
     gathers = [
         go(remote(inner_h, yr.at[y], y_s.at[dy], y_r.at[dy], at_y(dy))) for dy in range(1, NY)
     ]
@@ -150,7 +152,7 @@
     places = onehot(iota((128, 1024), 0).astype(F32) == lane)
     meta[0] = lax.dot_general(
         lines, places, (((1,), (1,)), ((), ())), preferred_element_type=F32
-    )
+    ).astype(BF16)
     metas = {}
     for way in (0, 1):
         metas[1, way] = go(meta_copy(1, way))
@@ -177,7 +179,7 @@
     def pick_rows(offset):
         p = POS[offset]
         line = (-offset) % NZ
-        wanted = meta[p][line : line + 1, :]
+        wanted = meta[p].astype(F32)[line : line + 1, :]
         take = onehot((iota((128, 128), 0) + 1).astype(F32) == wanted)
         rows = lax.dot_general(
             take, tok[p], (((0,), (0,)), ((), ())), preferred_element_type=F32
@@ -241,12 +243,12 @@
     loads[0].wait()
     pick_rows(0)
     for step in range(1, NZ // 2 + 1):
-        for half in (0, 1):
-            for way in ways(step, half):
-                ring[step, way, half].wait_recv()
-                if step < NZ // 2 and way in ways(step + 1, half):
-                    ring[step + 1, way, half] = go(token_copy(step + 1, way, half))
-            if half == 0:
+        for piece_no in range(PIECES):
+            for way in ways(step, piece_no):
+                ring[step, way, piece_no].wait_recv()
+                if step < NZ // 2 and way in ways(step + 1, piece_no):
+                    ring[step + 1, way, piece_no] = go(token_copy(step + 1, way, piece_no))
+            if piece_no == 0:
                 for way in ways(step, 0):
                     metas[step, way].wait_recv()
                     if step < NZ // 2 and way in ways(step + 1, 0):
@@ -299,17 +301,15 @@
                 out.start()
                 outs.append(out)
                 continue
-            for m in range(4):
-                rows = slice(256 * m, 256 * m + 256)
-                grads = jnp.dot(
-                    xt[e, rows, 256 * group : 256 * group + 256],
-                    gd[e, group],
-                    preferred_element_type=F32,
-                )
-                if group == FINISH[0]:
-                    acc[e, rows] = grads
-                else:
-                    some[e, rows] = (acc[e, rows] + grads).astype(BF16)
+            grads = jnp.dot(
+                xt[e, :, 256 * group : 256 * group + 256],
+                gd[e, group],
+                preferred_element_type=F32,
+            )
+            if group == FINISH[0]:
+                acc[e] = grads
+            else:
+                some[e] = (acc[e] + grads).astype(BF16)
             if group == FINISH[1]:
                 out = pltpu.make_async_copy(some.at[e], some_o.at[e], out_sem.at[2, e])
                 out.start()
@@ -320,15 +320,60 @@
         out.wait()
 
 
-def grad_kernel(x_ref, g_ref, some_ref, sum_ref, outer_ref, mom_ref, gate_ref, up_ref, no_ref, nm_ref):
-    grads = jnp.dot(x_ref[0], g_ref[0], preferred_element_type=F32)
-    grads = (grads + some_ref[0].astype(F32)).astype(BF16)
-    gate_ref[0] = grads[:, 0:384]
-    up_ref[0] = grads[:, 384:768]
-    delta = outer_ref[...] - sum_ref[...] / 16.0
-    momentum = 0.9 * mom_ref[...] + delta
-    nm_ref[...] = momentum
-    no_ref[...] = outer_ref[...] - 0.7 * (delta + 0.9 * momentum)
+def grad_kernel(
+    x_h, g_h, some_h, sum_h, outer_h, mom_h,
+    gate_o, up_o, outer_o, mom_o,
+    x, g, some, grads, steps, in_sem, g_sem, step_sem, out_sem,
+):
+    tile = 1024 // TILES
+    small = [
+        pltpu.make_async_copy(ref, steps.at[i], step_sem.at[i])
+        for i, ref in enumerate((sum_h, outer_h, mom_h))
+    ]
+    loads, g_loads = {}, []
+    for e in range(2):
+        g_loads.append(pltpu.make_async_copy(g_h.at[e], g.at[e], g_sem.at[e]))
+        g_loads[e].start()
+        for m in range(TILES):
+            rows = pl.ds(tile * m, tile)
+            loads[e, m] = (
+                pltpu.make_async_copy(x_h.at[e, rows], x.at[e, rows], in_sem.at[e, m, 0]),
+                pltpu.make_async_copy(some_h.at[e, rows], some.at[e, rows], in_sem.at[e, m, 1]),
+            )
+            for load in loads[e, m]:
+                load.start()
+        if e == 0:
+            for load in small:
+                load.start()
+    outs = []
+
+    def out(src, dst, sem):
+        outs.append(pltpu.make_async_copy(src, dst, sem))
+        outs[-1].start()
+
+    for e in range(2):
+        g_loads[e].wait()
+        for m in range(TILES):
+            rows = pl.ds(tile * m, tile)
+            for load in loads[e, m]:
+                load.wait()
+            total = jnp.dot(x[e, rows], g[e], preferred_element_type=F32)
+            total = (total + some[e, rows].astype(F32)).astype(BF16)
+            grads[0, e, rows] = total[:, 0:384]
+            grads[1, e, rows] = total[:, 384:768]
+            out(grads.at[0, e, rows], gate_o.at[e, rows], out_sem.at[e, m, 0])
+            out(grads.at[1, e, rows], up_o.at[e, rows], out_sem.at[e, m, 1])
+        if e == 0:
+            for load in small:
+                load.wait()
+            delta = steps[1] - steps[0] / 16.0
+            momentum = 0.9 * steps[2] + delta
+            steps[3] = steps[1] - 0.7 * (delta + 0.9 * momentum)
+            steps[4] = momentum
+            out(steps.at[3], outer_o, step_sem.at[3])
+            out(steps.at[4], mom_o, step_sem.at[4])
+    for copy in outs:
+        copy.wait()
 
 
 def local(tokens, ids, hidden, gate_weight, up_weight, outer, momentum, inner):
@@ -347,7 +392,7 @@
         out_specs=(any_, any_, any_, vmem),
         scratch_shapes=[
             pltpu.VMEM((NZ, 128, 1024), BF16),
-            pltpu.VMEM((NZ, 16, 128), F32),
+            pltpu.VMEM((NZ, 16, 128), BF16),
             pltpu.VMEM((NZ, 4, 2, ROWS, 1024), BF16),
             pltpu.VMEM((NZ, 4, 2, ROWS, 1024), BF16),
             pltpu.VMEM((2, 1024, 768), BF16),
@@ -363,7 +408,7 @@
             pltpu.VMEM((2, 1024, 768), BF16),
             pltpu.VMEM((NY, 8, 2048), F32),
             pltpu.VMEM((2, 8, 2048), F32),
-            dma((5,)), dma((NZ, 2)), dma((NZ, 2)), dma((NZ,)), dma((NZ,)),
+            dma((5,)), dma((NZ, PIECES)), dma((NZ, PIECES)), dma((NZ,)), dma((NZ,)),
             dma((NZ, 4)), dma((NZ, 4)), dma((3, 4)), dma((3, 4)), dma((NZ,)), dma((NZ,)),
             dma((NY,)), dma((NY,)), dma, dma, dma((3, 2)),
         ],
@@ -376,27 +421,22 @@
     )(ids[0].T, tokens[0], hidden[0].reshape(1024, 384), gate_weight, up_weight, inner[0])
     gate_grad, up_grad, new_outer, new_momentum = pl.pallas_call(
         grad_kernel,
-        grid=(2, 2),
         out_shape=(
             jax.ShapeDtypeStruct((2, 1024, 384), BF16),
             jax.ShapeDtypeStruct((2, 1024, 384), BF16),
             jax.ShapeDtypeStruct((8, 2048), F32),
             jax.ShapeDtypeStruct((8, 2048), F32),
         ),
-        in_specs=[
-            pl.BlockSpec((1, 512, 256), lambda e, m: (e, m, 0)),
-            pl.BlockSpec((1, 256, 768), lambda e, m: (e, 0, 0)),
-            pl.BlockSpec((1, 512, 768), lambda e, m: (e, m, 0)),
-            pl.BlockSpec((8, 2048), lambda e, m: (0, 0)),
-            pl.BlockSpec((8, 2048), lambda e, m: (0, 0)),
-            pl.BlockSpec((8, 2048), lambda e, m: (0, 0)),
+        in_specs=[any_] * 6,
+        out_specs=(any_,) * 4,
+        scratch_shapes=[
+            pltpu.VMEM((2, 1024, 256), BF16),
+            pltpu.VMEM((2, 256, 768), BF16),
+            pltpu.VMEM((2, 1024, 768), BF16),
+            pltpu.VMEM((2, 2, 1024, 384), BF16),
+            pltpu.VMEM((5, 8, 2048), F32),
+            dma((2, TILES, 2)), dma((2,)), dma((5,)), dma((2, TILES, 2)),
         ],
-        out_specs=(
-            pl.BlockSpec((1, 512, 384), lambda e, m: (e, m, 0)),
-            pl.BlockSpec((1, 512, 384), lambda e, m: (e, m, 0)),
-            pl.BlockSpec((8, 2048), lambda e, m: (0, 0)),
-            pl.BlockSpec((8, 2048), lambda e, m: (0, 0)),
-        ),
         compiler_params=pltpu.CompilerParams(vmem_limit_bytes=60 << 20),
     )(x_rows, g_rows, some, summed, outer, momentum)
     return gate_grad[None], up_grad[None], new_outer, new_momentum

time: 96.8 us -> 95.5 us (0.987)
  no operation moved by 1% of the time
where the time goes in v3:
time: 95.5 us; the launch traced here: 94.6 us
  Pallas kernels  94 us (98%)
    pallas_call x1, Pallas kernels, local(): pl.pallas_call(dispatch_kernel, out_shape=(jax.ShapeDtypeStruct((2, 1024,...  89.5 us
    pallas_call x1, Pallas kernels, local(): pl.pallas_call(grad_kernel, out_shape=(jax.ShapeDtypeStruct((2, 1024, 384...  4.48 us

profile of v3, /device:TPU:1, one launch (start us, length us, event | category | flops | bytes accessed | tf_op | source)
XLA Modules:
  0.0 94.6 jit_solution(5490760711752476719)
XLA Ops:
  0.6 89.5 %shard_map.111 = (bf16[2,1024,256]{2,1,0:T(8,128)(2,1)}, bf16[2,256,768]{2,1,0:T(8,128)(2,1)}, bf16[2,1024,768]{2,1,0:T(8,128)(2,1)}, f32[8,2048]{1,0:T(8,128)}) custom-call(s32[8,128]{1,0:T(8,128)} %bitcast.13, bf16[128,1024]{1,0:T(8,128)(2,1)} %bitcast.11, bf16[1024,384]{1,0:T(8,128)(2,1)} %bitcast.10, bf16[2,1024,384]{2,1,0:T(8,128)(2,1)} %gate_h.1, ...), custom_call_target="tpu_custom_call" | custom-call | flops 4000000000 | bytes 16000000 | tf_op jit(solution)/shard_map/pallas_call | solution.py:383
  90.1 4.5 %shard_map.112 = (bf16[2,1024,384]{2,1,0:T(8,128)(2,1)}, bf16[2,1024,384]{2,1,0:T(8,128)(2,1)}, f32[8,2048]{1,0:T(8,128)}, f32[8,2048]{1,0:T(8,128)}) custom-call(bf16[2,1024,256]{2,1,0:T(8,128)(2,1)} %get-tuple-element.12.x_h, bf16[2,256,768]{2,1,0:T(8,128)(2,1)} %get-tuple-element.13.g_h, bf16[2,1024,768]{2,1,0:T(8,128)(2,1)} %get-tuple-element.14.some_h, ...), custom_call_target="tpu_custom_call" | custom-call | tf_op jit(solution)/shard_map/pallas_call | solution.py:422

commit v4 on v3

--- a/solution.py
+++ b/solution.py
@@ -285,6 +285,10 @@
     target = iota((256, 4 * LINE), 0).astype(F32)
     goal = (at_p * 4.0 + at_s) * float(ROWS) + at_slot
     spaced = [onehot((target == goal) & (at_e == float(e))) for e in range(2)]
+    late = list(along.values())
+    for copy in sent:
+        if not any(copy is other for other in late):
+            copy.wait_send()
     for group in FINISH:
         for p in range(4 * group, 4 * group + 4):
             if p in along:
@@ -314,7 +318,7 @@
                 out = pltpu.make_async_copy(some.at[e], some_o.at[e], out_sem.at[2, e])
                 out.start()
                 outs.append(out)
-    for copy in sent:
+    for copy in late:
         copy.wait_send()
     for out in outs:
         out.wait()

time: 95.5 us -> 95.5 us (level)
  no operation moved by 1% of the time
where the time goes in v4:
time: 95.5 us; the launch traced here: 94.7 us
  Pallas kernels  94.1 us (99%)
    pallas_call x1, Pallas kernels, local(): pl.pallas_call(dispatch_kernel, out_shape=(jax.ShapeDtypeStruct((2, 1024,...  89.6 us
    pallas_call x1, Pallas kernels, local(): pl.pallas_call(grad_kernel, out_shape=(jax.ShapeDtypeStruct((2, 1024, 384...  4.48 us

profile of v4, /device:TPU:1, one launch (start us, length us, event | category | flops | bytes accessed | tf_op | source)
XLA Modules:
  0.0 94.7 jit_solution(7254031356181721807)
XLA Ops:
  0.6 89.6 %shard_map.111 = (bf16[2,1024,256]{2,1,0:T(8,128)(2,1)}, bf16[2,256,768]{2,1,0:T(8,128)(2,1)}, bf16[2,1024,768]{2,1,0:T(8,128)(2,1)}, f32[8,2048]{1,0:T(8,128)}) custom-call(s32[8,128]{1,0:T(8,128)} %bitcast.13, bf16[128,1024]{1,0:T(8,128)(2,1)} %bitcast.11, bf16[1024,384]{1,0:T(8,128)(2,1)} %bitcast.10, bf16[2,1024,384]{2,1,0:T(8,128)(2,1)} %gate_h.1, ...), custom_call_target="tpu_custom_call" | custom-call | flops 4000000000 | bytes 16000000 | tf_op jit(solution)/shard_map/pallas_call | solution.py:387
  90.3 4.5 %shard_map.112 = (bf16[2,1024,384]{2,1,0:T(8,128)(2,1)}, bf16[2,1024,384]{2,1,0:T(8,128)(2,1)}, f32[8,2048]{1,0:T(8,128)}, f32[8,2048]{1,0:T(8,128)}) custom-call(bf16[2,1024,256]{2,1,0:T(8,128)(2,1)} %get-tuple-element.12.x_h, bf16[2,256,768]{2,1,0:T(8,128)(2,1)} %get-tuple-element.13.g_h, bf16[2,1024,768]{2,1,0:T(8,128)(2,1)} %get-tuple-element.14.some_h, ...), custom_call_target="tpu_custom_call" | custom-call | tf_op jit(solution)/shard_map/pallas_call | solution.py:426

commit v5 on v3

--- a/solution.py
+++ b/solution.py
@@ -13,7 +13,7 @@
 ARRIVAL = [0, 1, 11, 2, 10, 3, 9, 4, 8, 5, 7, 6]
 POS = {o: p for p, o in enumerate(ARRIVAL)}
 FAR = [6, 5, 7, 4, 8, 3, 9, 2, 10, 1, 11, 0]
-LEAVE = (4, 4, 5, 5, 5, 5, 5, 6, 6, 6, 6, 6)
+LEAVE = (4, 4, 4, 4, 5, 5, 5, 5, 5, 5, 5, 5)
 FINISH = (2, 1, 0)
 PAIR = 28
 LINE = 4 * PAIR

time: 95.5 us -> 99.5 us (1.042)
  Pallas kernels: 94 us -> 98.7 us
    pallas_call x1, Pallas kernels: 89.5 us -> 94.2 us  [local(): pl.pallas_call(dispatch_kernel, out_shape=(jax.ShapeDtypeStruct((2, 1024,...]
where the time goes in v5:
time: 99.5 us; the launch traced here: 99.3 us
  Pallas kernels  98.7 us (99%)
    pallas_call x1, Pallas kernels, local(): pl.pallas_call(dispatch_kernel, out_shape=(jax.ShapeDtypeStruct((2, 1024,...  94.2 us
    pallas_call x1, Pallas kernels, local(): pl.pallas_call(grad_kernel, out_shape=(jax.ShapeDtypeStruct((2, 1024, 384...  4.48 us

profile of v5, /device:TPU:1, one launch (start us, length us, event | category | flops | bytes accessed | tf_op | source)
XLA Modules:
  0.0 99.3 jit_solution(9547830049721003848)
XLA Ops:
  0.6 94.2 %shard_map.111 = (bf16[2,1024,256]{2,1,0:T(8,128)(2,1)}, bf16[2,256,768]{2,1,0:T(8,128)(2,1)}, bf16[2,1024,768]{2,1,0:T(8,128)(2,1)}, f32[8,2048]{1,0:T(8,128)}) custom-call(s32[8,128]{1,0:T(8,128)} %bitcast.13, bf16[128,1024]{1,0:T(8,128)(2,1)} %bitcast.11, bf16[1024,384]{1,0:T(8,128)(2,1)} %bitcast.10, bf16[2,1024,384]{2,1,0:T(8,128)(2,1)} %gate_h.1, ...), custom_call_target="tpu_custom_call" | custom-call | flops 4000000000 | bytes 16000000 | tf_op jit(solution)/shard_map/pallas_call | solution.py:383
  94.8 4.5 %shard_map.112 = (bf16[2,1024,384]{2,1,0:T(8,128)(2,1)}, bf16[2,1024,384]{2,1,0:T(8,128)(2,1)}, f32[8,2048]{1,0:T(8,128)}, f32[8,2048]{1,0:T(8,128)}) custom-call(bf16[2,1024,256]{2,1,0:T(8,128)(2,1)} %get-tuple-element.12.x_h, bf16[2,256,768]{2,1,0:T(8,128)(2,1)} %get-tuple-element.13.g_h, bf16[2,1024,768]{2,1,0:T(8,128)(2,1)} %get-tuple-element.14.some_h, ...), custom_call_target="tpu_custom_call" | custom-call | tf_op jit(solution)/shard_map/pallas_call | solution.py:422
